TPU v7x, 32 devices: a whole 2x2x4 slice. The times are simulated.
32 devices in a mesh: dom: 4 (over z), feat: 8 (over y, x, core).
Axes of the slice: x: 2, y: 2, z: 4, core: 2. Of those that a mesh axis runs over, the one named last changes fastest.
Arguments:
- features: bfloat16 [4096, 4096], P('dom', 'feat'), may hold values from -6 to 6
- proj_weight: bfloat16 [3, 4096, 256], P(None, 'feat'), may hold values from -0.75 to 0.75
- source_block: int32 [32, 3, 4], P('dom'), may hold values from 0 to 7
- slot_count: int32 [32, 3], P('dom'), may hold values from 1 to 4
- block_pattern: int32 [32, 3, 4, 8, 128], P('dom'), may hold values from 0 to 65535
- node_type: int32 [4096], P(('dom', 'feat')), may hold values from 0 to 2
- type_gain: float32 [3, 256], replicated, may hold values from 0.1 to 1.9
- cotangent: bfloat16 [4096, 256], P(('dom', 'feat')), may hold values from -6 to 6
Outputs:
- activations: bfloat16 [4096, 256], P(('dom', 'feat'))
- weight_grad: float32 [3, 4096, 256], P(None, 'feat')
Inputs may be any that keep to these rules, and one draw needn't show every extreme that they name: `source_block`: a block index within the destination block's own partition. `slot_count`: slots at or past this count are ignored. `block_pattern`: bit j of the word at index w, i marks an edge from source node 16 w + j of the slot's block to node i of the destination block.
All inputs are finite; a program needn't handle non-finite values.
Results may differ from a plain program's by a relative error of at most 0.0055.
Values may be sent and summed in bfloat16 or wider, within the bound.
No kernel may reach another device: no remote copies, remote signals or barrier semaphores. Data moves between devices by JAX's collectives and lax.ppermute only.
A program may use at most 128 MiB of HBM per device.

v0:
```python
import functools

import jax
import jax.numpy as jnp
from jax import lax
from jax.experimental import pallas as pl
from jax.experimental.pallas import tpu as pltpu
from jax.sharding import PartitionSpec as P

BLK = 128
MIB = 1024 * 1024
BF16 = jnp.bfloat16
F32 = jnp.float32


def unpack_bits(packed):
    shifts = (2 ** jnp.arange(16)).astype(jnp.int32)
    bit_values = packed[..., None] // shifts % 2
    bit_values = jnp.swapaxes(bit_values, -3, -2)
    return bit_values.reshape(packed.shape[:-2] + (packed.shape[-1], packed.shape[-2] * 16))


def silu_grad(pre_act):
    sigmoid_value = jax.nn.sigmoid(pre_act)
    return sigmoid_value * (1.0 + pre_act * (1.0 - sigmoid_value))


def type_rows(node_type, type_gain):
    onehot = (
        node_type[:, None] == jnp.arange(type_gain.shape[0], dtype=jnp.int32)[None, :]
    ).astype(jnp.float32)
    return jnp.sum(onehot[:, :, None] * type_gain[None, :, :], axis=1)


def aggregate(features, source_block, slot_count, block_pattern):
    count_blocks = source_block.shape[0]
    relations = source_block.shape[1]
    slots_each = source_block.shape[2]
    col_width = features.shape[1]
    blocks = features.reshape(count_blocks, BLK, col_width)
    blocks_wide = blocks.astype(jnp.float32)
    live_slots = (
        jnp.arange(slots_each, dtype=jnp.int32)[None, None, :] < slot_count[:, :, None]
    ).astype(jnp.float32)
    mixed_list = []
    for relation in range(relations):
        summed = jnp.zeros((count_blocks, BLK, col_width), jnp.float32)
        degree = jnp.zeros((count_blocks, BLK), jnp.float32)
        for slot_index in range(slots_each):
            adjacency = (
                unpack_bits(block_pattern[:, relation, slot_index]).astype(jnp.float32)
                * live_slots[:, relation, slot_index][:, None, None]
            )
            picked = jnp.take(blocks, source_block[:, relation, slot_index], axis=0)
            summed = summed + jnp.einsum(
                "bij,bjc->bic",
                adjacency.astype(jnp.bfloat16),
                picked,
                preferred_element_type=jnp.float32,
            )
            degree = degree + jnp.sum(adjacency, axis=2)
        mixed_rows = ((blocks_wide + summed) / (1.0 + degree)[:, :, None]).astype(jnp.bfloat16)
        mixed_list.append(mixed_rows.reshape(count_blocks * BLK, col_width))
    return jnp.stack(mixed_list)


def general_body(
    features, proj_weight, source_block, slot_count, block_pattern, node_type, type_gain, cotangent
):
    mixed_all = aggregate(features, source_block, slot_count, block_pattern)
    pre_act = lax.psum_scatter(
        jnp.einsum("rnc,rch->nh", mixed_all, proj_weight, preferred_element_type=jnp.float32),
        "feat",
        scatter_dimension=0,
        tiled=True,
    )
    row_gains = type_rows(node_type, type_gain)
    output = (jax.nn.silu(pre_act) * row_gains).astype(jnp.bfloat16)
    slope_rows = (cotangent.astype(jnp.float32) * row_gains * silu_grad(pre_act)).astype(
        jnp.bfloat16
    )
    local_grad = jnp.einsum(
        "rnc,nh->rch",
        mixed_all,
        lax.all_gather(slope_rows, "feat", axis=0, tiled=True),
        preferred_element_type=jnp.float32,
    )
    weight_grad = lax.psum(local_grad, "dom")
    return (output, weight_grad)


def forward_kernel(
    src_ref, cnt_ref, pat_hbm, x_hbm, w_hbm, inv_ref, out_ref, *rest
):
    relations, slots, blocks = src_ref.shape
    adj_out = rest[:relations]
    pat_ref, x_ref, w_ref, adj_ref, pre_ref, in_sem, out_sem = rest[relations:]

    loads = [
        pltpu.make_async_copy(pat_hbm, pat_ref, in_sem.at[0]),
        pltpu.make_async_copy(x_hbm, x_ref, in_sem.at[1]),
        pltpu.make_async_copy(w_hbm, w_ref, in_sem.at[2]),
    ]
    for load in loads:
        load.start()
    loads[0].wait()

    sub = lax.broadcasted_iota(jnp.int32, (BLK, BLK), 0)
    lane = lax.broadcasted_iota(jnp.int32, (BLK, BLK), 1)
    eye = jnp.where(sub == lane, 1.0, 0.0).astype(BF16)
    bit = jnp.left_shift(1, lax.broadcasted_iota(jnp.int32, (16, BLK), 0))

    def build(relation):
        adj_r = adj_ref.at[relation]
        adj_r[...] = jnp.zeros(adj_r.shape, BF16)
        for b in range(blocks):
            cols = pl.ds(b * BLK, BLK)
            adj_r[b * BLK : (b + 1) * BLK, cols] = eye
            count = cnt_ref[relation, b]
            degree = jnp.zeros((8, BLK), jnp.int32)
            for s in range(slots):
                live = jnp.where(s < count, 0xFFFF, 0)
                words = pat_ref[b, relation, s] & live
                row0 = pl.multiple_of(src_ref[relation, s, b] * BLK, BLK)
                parts = [
                    jnp.where((words[w : w + 1, :] & bit) != 0, 1.0, 0.0)
                    for w in range(words.shape[0])
                ]
                tile = jnp.concatenate(parts, axis=0).astype(BF16)
                adj_r[pl.ds(row0, BLK), cols] += tile
                c = words - ((words >> 1) & 0x5555)
                c = (c & 0x3333) + ((c >> 2) & 0x3333)
                c = (c + (c >> 4)) & 0x0F0F
                degree = degree + ((c + (c >> 8)) & 0x1F)
            total = jnp.sum(degree.astype(F32), axis=0, keepdims=True)
            inv_ref[relation, 0:1, cols] = 1.0 / (1.0 + total)

    stores = []
    for relation in range(relations):
        build(relation)
        store = pltpu.make_async_copy(
            adj_ref.at[relation], adj_out[relation], out_sem.at[relation]
        )
        store.start()
        stores.append(store)
        if relation == 0:
            loads[1].wait()
            loads[2].wait()
        w_t = w_ref[relation].T
        y_t = lax.dot_general(
            w_t, x_ref[...], (((1,), (1,)), ((), ())), preferred_element_type=F32
        ).astype(BF16)
        p_t = jnp.dot(y_t, adj_ref[relation], preferred_element_type=F32)
        p_t = p_t * inv_ref[relation, 0:1, :]
        if relation == 0:
            pre_ref[...] = p_t
        else:
            pre_ref[...] += p_t

    for b in range(blocks):
        rows = slice(b * BLK, (b + 1) * BLK)
        out_ref[rows, :] = pre_ref[:, rows].T.astype(BF16)
    for store in stores:
        store.wait()


def forward(features, proj_weight, source_block, slot_count, block_pattern):
    nodes, cols = features.shape
    relations, _, hidden = proj_weight.shape
    hbm = pl.BlockSpec(memory_space=pltpu.HBM)
    smem = pl.BlockSpec(memory_space=pltpu.SMEM)
    vmem = pl.BlockSpec(memory_space=pltpu.VMEM)
    inv_deg, partial, *adj = pl.pallas_call(
        forward_kernel,
        name="forward",
        out_shape=[
            jax.ShapeDtypeStruct((relations, 8, nodes), F32),
            jax.ShapeDtypeStruct((nodes, hidden), BF16),
        ]
        + [jax.ShapeDtypeStruct((nodes, nodes), BF16)] * relations,
        in_specs=[smem, smem, hbm, hbm, hbm],
        out_specs=[vmem, vmem] + [hbm] * relations,
        scratch_shapes=[
            pltpu.VMEM(block_pattern.shape, jnp.int32),
            pltpu.VMEM(features.shape, BF16),
            pltpu.VMEM(proj_weight.shape, BF16),
            pltpu.VMEM((relations, nodes, nodes), BF16),
            pltpu.VMEM((hidden, nodes), F32),
            pltpu.SemaphoreType.DMA((3,)),
            pltpu.SemaphoreType.DMA((relations,)),
        ],
        compiler_params=pltpu.CompilerParams(vmem_limit_bytes=64 * MIB),
    )(
        jnp.transpose(source_block, (1, 2, 0)),
        jnp.transpose(slot_count, (1, 0)),
        block_pattern,
        features,
        proj_weight,
    )
    return inv_deg, partial, adj


def prepare_kernel(x_ref, inv_ref, xt_ref, *col_refs):
    nodes = x_ref.shape[0]
    for b in range(nodes // BLK):
        rows = slice(b * BLK, (b + 1) * BLK)
        xt_ref[:, rows] = x_ref[rows, :].T
        for r, col_ref in enumerate(col_refs):
            wide = jnp.broadcast_to(inv_ref[r, 0:1, rows], (BLK, BLK))
            col_ref[rows, :] = wide.T


def prepare(features, inv_deg):
    nodes, cols = features.shape
    relations = inv_deg.shape[0]
    x_t, *col = pl.pallas_call(
        prepare_kernel,
        name="prepare",
        out_shape=[jax.ShapeDtypeStruct((cols, nodes), BF16)]
        + [jax.ShapeDtypeStruct((nodes, BLK), F32)] * relations,
        compiler_params=pltpu.CompilerParams(vmem_limit_bytes=12 * MIB),
        cost_estimate=pl.CostEstimate(
            flops=2 * nodes * cols, bytes_accessed=6 * nodes * cols, transcendentals=0
        ),
    )(features, inv_deg)
    return x_t, col


def combine_kernel(n_feat, part_ref, type_ref, gain_ref, cot_ref, act_ref, slope_ref):
    rows = act_ref.shape[0]
    pre = part_ref[0:rows, :].astype(F32)
    for k in range(1, n_feat):
        pre = pre + part_ref[k * rows : (k + 1) * rows, :].astype(F32)
    types = jnp.broadcast_to(type_ref[...].astype(F32), (rows, rows)).T
    types = jnp.concatenate([types] * (act_ref.shape[1] // rows), axis=1)
    gain = jnp.zeros(act_ref.shape, F32)
    for t in range(gain_ref.shape[0]):
        gain = jnp.where(types == t, gain_ref[t : t + 1, :], gain)
    sig = jax.nn.sigmoid(pre)
    act_ref[...] = (pre * sig * gain).astype(BF16)
    grad = sig * (1.0 + pre * (1.0 - sig))
    slope_ref[...] = (cot_ref[...].astype(F32) * gain * grad).astype(BF16)


def combine(partial, node_type, type_gain, cotangent, n_feat):
    shape = jax.ShapeDtypeStruct(cotangent.shape, BF16)
    return pl.pallas_call(
        functools.partial(combine_kernel, n_feat),
        name="combine",
        out_shape=[shape, shape],
        compiler_params=pltpu.CompilerParams(vmem_limit_bytes=6 * MIB),
    )(partial, node_type[None, :], type_gain, cotangent)


def gradient_kernel(
    xt_ref, adj_ref, col_ref, slope_ref, wide_ref, sent_ref, scaled_ref
):
    inv = col_ref[...]
    inv = jnp.concatenate([inv] * (slope_ref.shape[1] // BLK), axis=1)
    scaled_ref[...] = (slope_ref[...].astype(F32) * inv).astype(BF16)
    spread = jnp.dot(adj_ref[...], scaled_ref[...], preferred_element_type=F32).astype(BF16)
    grad = jnp.dot(xt_ref[...], spread, preferred_element_type=F32)
    wide_ref[...] = grad
    sent_ref[...] = grad.astype(BF16)


def gradient(x_t, adj, col, slopes):
    cols, nodes = x_t.shape
    hidden = slopes.shape[1]
    vmem = pl.BlockSpec(memory_space=pltpu.VMEM)
    return pl.pallas_call(
        gradient_kernel,
        name="gradient",
        out_shape=[
            jax.ShapeDtypeStruct((cols, hidden), F32),
            jax.ShapeDtypeStruct((cols, hidden), BF16),
        ],
        in_specs=[vmem] * 4,
        out_specs=[vmem] * 2,
        scratch_shapes=[
            pltpu.VMEM((nodes, hidden), BF16),
        ],
        compiler_params=pltpu.CompilerParams(vmem_limit_bytes=12 * MIB),
        cost_estimate=pl.CostEstimate(
            flops=2 * nodes * hidden * (nodes + cols),
            bytes_accessed=2 * nodes * nodes + 6 * cols * hidden,
            transcendentals=0,
        ),
    )(x_t, adj, col, slopes)


def rounded(x):
    return lax.reduce_precision(x, 8, 7)


def chain_sum(wide, sent, n_dom):
    half = n_dom // 2
    at = lax.axis_index("dom")
    total = wide
    for hop in range(half - 1):
        perm = [(hop, hop + 1), (n_dom - 1 - hop, n_dom - 2 - hop)]
        total = rounded(total + lax.ppermute(sent, "dom", perm).astype(F32))
        sent = total.astype(BF16)
    got = lax.ppermute(sent, "dom", [(half - 1, half), (half, half - 1)])
    total = rounded(sent.astype(F32) + got.astype(F32))
    sent = total.astype(BF16)
    for hop in range(half - 1):
        low, high = half - 1 - hop, half + hop
        got = lax.ppermute(sent, "dom", [(low, low - 1), (high, high + 1)])
        outside = (at < low) | (at > high)
        sent = jnp.where(outside, got, sent)
    return sent.astype(F32)


def dense_body(
    n_dom,
    n_feat,
    features,
    proj_weight,
    source_block,
    slot_count,
    block_pattern,
    node_type,
    type_gain,
    cotangent,
):
    relations = proj_weight.shape[0]
    inv_deg, partial, adj = forward(
        features, proj_weight, source_block, slot_count, block_pattern
    )
    parts = lax.all_to_all(partial, "feat", 0, 0, tiled=True)
    x_t, col = prepare(features, inv_deg)
    activations, slope = combine(parts, node_type, type_gain, cotangent, n_feat)
    slopes = lax.all_gather(slope, "feat", axis=0, tiled=True)
    grads = []
    for relation in range(relations):
        wide, sent = gradient(x_t, adj[relation], col[relation], slopes)
        grads.append(chain_sum(wide, sent, n_dom))
    return activations, jnp.stack(grads)


def body(n_dom, n_feat, *args):
    features, source_block = args[0], args[2]
    nodes = features.shape[0]
    fits = 2 * source_block.shape[1] * nodes * nodes <= 8 * MIB
    pairs_up = n_feat & (n_feat - 1) == 0 and n_dom % 2 == 0
    if fits and pairs_up and nodes == n_feat * BLK:
        return dense_body(n_dom, n_feat, *args)
    return general_body(*args)


def solution(mesh):
    placed = (
        P("dom", "feat"),
        P(None, "feat", None),
        P("dom", None, None),
        P("dom", None),
        P("dom", None, None, None, None),
        P(("dom", "feat")),
        P(),
        P(("dom", "feat"), None),
    )
    return jax.shard_map(
        functools.partial(body, mesh.shape["dom"], mesh.shape["feat"]),
        mesh=mesh,
        in_specs=placed,
        out_specs=(P(("dom", "feat"), None), P(None, "feat", None)),
        check_vma=False,
    )
```

profile of v0, /device:TPU:0, one launch (start us, length us, event | category | flops | bytes accessed | tf_op | source)
XLA Modules:
  0.0 83.6 jit_solution(16631679206813792639)
XLA Ops:
  0.6 7.6 %forward.1 = (f32[3,8,1024]{2,1,0:T(8,128)}, bf16[1024,256]{1,0:T(8,128)(2,1)}, bf16[1024,1024]{1,0:T(8,128)(2,1)}, bf16[1024,1024]{1,0:T(8,128)(2,1)}, bf16[1024,1024]{1,0:T(8,128)(2,1)}) custom-call(s32[3,4,8]{2,1,0:T(4,128)} %bitcast.14, s32[3,8]{1,0:T(4,128)} %bitcast.15, s32[8,3,4,8,128]{4,3,2,1,0:T(8,128)} %pat_hbm.1, bf16[1024,512]{1,0:T(8,128)(2,1)} %x_ref.1, ...), custom_call_target="tpu_custom_call" | custom-call | tf_op jit(solution)/shard_map/forward/pallas_call | solution.py:173
  8.3 0.0 copy-start.7
  8.3 0.0 copy-start.8
  8.3 0.0 copy-start.9
  8.3 5.3 %all-to-all-start = ((bf16[8,128,256]{2,1,0:T(8,128)(2,1)}), bf16[8,128,256]{2,1,0:T(8,128)(2,1)S(1)}, u32[]{:S(2)}, u32[]{:S(2)}) async-start(bf16[8,128,256]{2,1,0:T(8,128)(2,1)} %bitcast.13), calls=%async_computation | async-start | bytes 1048576 | tf_op jit(solution)/shard_map/all_to_all | solution.py:331
  13.6 1.2 %copy-done = bf16[1024,512]{1,0:T(8,128)(2,1)S(1)} copy-done((bf16[1024,512]{1,0:T(8,128)(2,1)S(1)}, bf16[1024,512]{1,0:T(8,128)(2,1)}, u32[]{:S(2)}) %copy-start) | copy-done | bytes 1048600
  14.9 0.9 %copy-done.6 = f32[3,8,1024]{2,1,0:T(8,128)S(1)} copy-done((f32[3,8,1024]{2,1,0:T(8,128)S(1)}, f32[3,8,1024]{2,1,0:T(8,128)}, u32[]{:S(2)}) %copy-start.6) | copy-done | bytes 98328
  15.7 0.9 %prepare.1 = (bf16[512,1024]{1,0:T(8,128)(2,1)S(1)}, f32[1024,128]{1,0:T(8,128)S(1)}, f32[1024,128]{1,0:T(8,128)S(1)}, f32[1024,128]{1,0:T(8,128)S(1)}) custom-call(bf16[1024,512]{1,0:T(8,128)(2,1)S(1)} %copy-done, f32[3,8,1024]{2,1,0:T(8,128)S(1)} %copy-done.6), custom_call_target="tpu_custom_call" | custom-call | flops 1048576 | bytes 3145728 | tf_op jit(solution)/shard_map/prepare/pallas_call | solution.py:216
  16.6 0.0 copy-start.4
  16.6 6.7 %all-to-all-done = bf16[8,128,256]{2,1,0:T(8,128)(2,1)S(1)} async-done(((bf16[8,128,256]{2,1,0:T(8,128)(2,1)}), bf16[8,128,256]{2,1,0:T(8,128)(2,1)S(1)}, u32[]{:S(2)}, u32[]{:S(2)}) %all-to-all-start) | async-done | bytes 524320 | tf_op jit(solution)/shard_map/all_to_all | solution.py:331
  23.4 0.0 copy-done.7
  23.4 0.0 copy-done.8
  23.4 0.0 copy-done.9
  23.4 0.8 combine.1
  24.2 8.9 %all_gather.3.slope_ref = bf16[1024,256]{1,0:T(8,128)(2,1)S(1)} all-gather(bf16[128,256]{1,0:T(8,128)(2,1)S(1)} %get-tuple-element.25), channel_id=1, replica_groups=mesh['dom'=4,'feat'=8] {'feat'}, dimensions={0}, use_global_device_ids=true | all-gather | bytes 589824 | tf_op jit(solution)/shard_map/all_gather | solution.py:334
  33.1 0.0 copy-done.4
  33.1 1.6 %copy-done.3 = bf16[1024,1024]{1,0:T(8,128)(2,1)S(1)} copy-done((bf16[1024,1024]{1,0:T(8,128)(2,1)S(1)}, bf16[1024,1024]{1,0:T(8,128)(2,1)}, u32[]{:S(2)}) %copy-start.3) | copy-done | bytes 2097176
  34.7 1.0 %copy-done.5 = f32[1024,128]{1,0:T(8,128)S(1)} copy-done((f32[1024,128]{1,0:T(8,128)S(1)}, f32[1024,128]{1,0:T(8,128)}, u32[]{:S(2)}) %copy-start.5) | copy-done | bytes 524312
  35.7 1.4 %gradient.5 = (f32[512,256]{1,0:T(8,128)S(1)}, bf16[512,256]{1,0:T(8,128)(2,1)S(1)}) custom-call(bf16[512,1024]{1,0:T(8,128)(2,1)S(1)} %get-tuple-element.22.xt_ref, bf16[1024,1024]{1,0:T(8,128)(2,1)S(1)} %copy-done.3, f32[1024,128]{1,0:T(8,128)S(1)} %copy-done.5, bf16[1024,256]{1,0:T(8,128)(2,1)S(1)} %all_gather.3.slope_ref), custom_call_target="tpu_custom_call" | custom-call | flops 805306368 | bytes 2883584 | tf_op jit(solution)/shard_map/gradient/pallas_call | solution.py:271
  37.1 4.2 %collective-permute-start.6 = (bf16[512,256]{1,0:T(8,128)(2,1)S(1)}, bf16[512,256]{1,0:T(8,128)(2,1)}, u32[]{:S(2)}, u32[]{:S(2)}) collective-permute-start(bf16[512,256]{1,0:T(8,128)(2,1)S(1)} %get-tuple-element.35), channel_id=1, source_target_pairs={{0,8},{24,16},{1,9},{25,17},{2,10},{26,18},{3,11},{27,19},{4,12},{... | collective-permute-start | bytes 786440 | tf_op jit(solution)/shard_map/ppermute | solution.py:302
  41.3 1.6 %copy-done.2 = bf16[1024,1024]{1,0:T(8,128)(2,1)S(1)} copy-done((bf16[1024,1024]{1,0:T(8,128)(2,1)S(1)}, bf16[1024,1024]{1,0:T(8,128)(2,1)}, u32[]{:S(2)}) %copy-start.2) | copy-done | bytes 2097176
  42.9 1.4 %gradient.4 = (f32[512,256]{1,0:T(8,128)S(1)}, bf16[512,256]{1,0:T(8,128)(2,1)S(1)}) custom-call(bf16[512,1024]{1,0:T(8,128)(2,1)S(1)} %get-tuple-element.22.xt_ref, bf16[1024,1024]{1,0:T(8,128)(2,1)S(1)} %copy-done.2, f32[1024,128]{1,0:T(8,128)S(1)} %get-tuple-element.29.col_ref, bf16[1024,256]{1,0:T(8,128)(2,1)S(1)} %all_gather.3.slope_ref), custom_call_target="tpu_custom_call" | custom-call | flops 805306368 | bytes 2883584 | tf_op jit(solution)/shard_map/gradient/pallas_call | solution.py:271
  44.3 1.3 %collective-permute-start.3 = (bf16[512,256]{1,0:T(8,128)(2,1)S(1)}, bf16[512,256]{1,0:T(8,128)(2,1)S(1)}, u32[]{:S(2)}, u32[]{:S(2)}) collective-permute-start(bf16[512,256]{1,0:T(8,128)(2,1)S(1)} %get-tuple-element.31), channel_id=1, source_target_pairs={{0,8},{24,16},{1,9},{25,17},{2,10},{26,18},{3,11},{27,19},{4,12},{... | collective-permute-start | bytes 786440 | tf_op jit(solution)/shard_map/ppermute | solution.py:302
  45.7 0.0 copy-done.1
  45.7 1.4 %gradient.3 = (f32[512,256]{1,0:T(8,128)S(1)}, bf16[512,256]{1,0:T(8,128)(2,1)S(1)}) custom-call(bf16[512,1024]{1,0:T(8,128)(2,1)S(1)} %get-tuple-element.22.xt_ref, bf16[1024,1024]{1,0:T(8,128)(2,1)S(1)} %copy-done.1, f32[1024,128]{1,0:T(8,128)S(1)} %get-tuple-element.24.col_ref, bf16[1024,256]{1,0:T(8,128)(2,1)S(1)} %all_gather.3.slope_ref), custom_call_target="tpu_custom_call" | custom-call | flops 805306368 | bytes 2883584 | tf_op jit(solution)/shard_map/gradient/pallas_call | solution.py:271
  47.1 1.3 %collective-permute-start = (bf16[512,256]{1,0:T(8,128)(2,1)S(1)}, bf16[512,256]{1,0:T(8,128)(2,1)S(1)}, u32[]{:S(2)}, u32[]{:S(2)}) collective-permute-start(bf16[512,256]{1,0:T(8,128)(2,1)S(1)} %get-tuple-element.27), channel_id=1, source_target_pairs={{0,8},{24,16},{1,9},{25,17},{2,10},{26,18},{3,11},{27,19},{4,12},{... | collective-permute-start | bytes 786440 | tf_op jit(solution)/shard_map/ppermute | solution.py:302
  48.4 0.0 collective-permute-done.6
  48.4 1.0 %reduce-precision_convert_fusion.1 = bf16[512,256]{1,0:T(8,128)(2,1)S(1)} fusion(f32[512,256]{1,0:T(8,128)S(1)} %get-tuple-element.34, bf16[512,256]{1,0:T(8,128)(2,1)} %collective-permute-done.6), kind=kLoop, calls=%fused_computation.2 | loop fusion | flops 524288 | bytes 1048576 | tf_op jit(solution)/shard_map/convert_element_type | solution.py:303
  49.4 0.7 collective-permute-start.7
  50.1 2.7 %collective-permute-done.3 = bf16[512,256]{1,0:T(8,128)(2,1)S(1)} collective-permute-done((bf16[512,256]{1,0:T(8,128)(2,1)S(1)}, bf16[512,256]{1,0:T(8,128)(2,1)S(1)}, u32[]{:S(2)}, u32[]{:S(2)}) %collective-permute-start.3) | collective-permute-done | bytes 262176 | tf_op jit(solution)/shard_map/ppermute | solution.py:302
  52.9 0.1 reduce-precision_convert_fusion.3
  52.9 0.7 collective-permute-start.4
  53.6 4.3 %collective-permute-done = bf16[512,256]{1,0:T(8,128)(2,1)S(1)} collective-permute-done((bf16[512,256]{1,0:T(8,128)(2,1)S(1)}, bf16[512,256]{1,0:T(8,128)(2,1)S(1)}, u32[]{:S(2)}, u32[]{:S(2)}) %collective-permute-start) | collective-permute-done | bytes 262176 | tf_op jit(solution)/shard_map/ppermute | solution.py:302
  57.9 0.1 reduce-precision_convert_fusion.5
  58.0 0.7 collective-permute-start.1
  58.7 0.0 collective-permute-done.7
  58.7 0.1 reduce-precision_convert_fusion
  58.7 1.3 %collective-permute-start.8 = (bf16[512,256]{1,0:T(8,128)(2,1)S(1)}, bf16[512,256]{1,0:T(8,128)(2,1)S(1)}, u32[]{:S(2)}, u32[]{:S(2)}) collective-permute-start(bf16[512,256]{1,0:T(8,128)(2,1)S(1)} %reduce-precision_convert_fusion), channel_id=1, source_target_pairs={{8,0},{16,24},{9,1},{17,25},{10,2},{18,26},{11,3},{19,27},{12,4},{... | collective-permute-start | bytes 786440 | tf_op jit(solution)/shard_map/ppermute | solution.py:309
  60.0 0.0 collective-permute-done.4
  60.1 0.1 reduce-precision_convert_fusion.2
  60.1 1.3 %collective-permute-start.5 = (bf16[512,256]{1,0:T(8,128)(2,1)S(1)}, bf16[512,256]{1,0:T(8,128)(2,1)S(1)}, u32[]{:S(2)}, u32[]{:S(2)}) collective-permute-start(bf16[512,256]{1,0:T(8,128)(2,1)S(1)} %reduce-precision_convert_fusion.2), channel_id=1, source_target_pairs={{8,0},{16,24},{9,1},{17,25},{10,2},{18,26},{11,3},{19,27},{12,4},{... | collective-permute-start | bytes 786440 | tf_op jit(solution)/shard_map/ppermute | solution.py:309
  61.4 0.0 collective-permute-done.1
  61.4 0.1 reduce-precision_convert_fusion.4
  61.5 1.3 %collective-permute-start.2 = (bf16[512,256]{1,0:T(8,128)(2,1)S(1)}, bf16[512,256]{1,0:T(8,128)(2,1)S(1)}, u32[]{:S(2)}, u32[]{:S(2)}) collective-permute-start(bf16[512,256]{1,0:T(8,128)(2,1)S(1)} %reduce-precision_convert_fusion.4), channel_id=1, source_target_pairs={{8,0},{16,24},{9,1},{17,25},{10,2},{18,26},{11,3},{19,27},{12,4},{... | collective-permute-start | bytes 786440 | tf_op jit(solution)/shard_map/ppermute | solution.py:309
  62.8 9.7 %collective-permute-done.8 = bf16[512,256]{1,0:T(8,128)(2,1)S(1)} collective-permute-done((bf16[512,256]{1,0:T(8,128)(2,1)S(1)}, bf16[512,256]{1,0:T(8,128)(2,1)S(1)}, u32[]{:S(2)}, u32[]{:S(2)}) %collective-permute-start.8) | collective-permute-done | bytes 262176 | tf_op jit(solution)/shard_map/ppermute | solution.py:309
  72.6 5.6 %collective-permute-done.5 = bf16[512,256]{1,0:T(8,128)(2,1)S(1)} collective-permute-done((bf16[512,256]{1,0:T(8,128)(2,1)S(1)}, bf16[512,256]{1,0:T(8,128)(2,1)S(1)}, u32[]{:S(2)}, u32[]{:S(2)}) %collective-permute-start.5) | collective-permute-done | bytes 262176 | tf_op jit(solution)/shard_map/ppermute | solution.py:309
  78.2 4.1 %collective-permute-done.2 = bf16[512,256]{1,0:T(8,128)(2,1)S(1)} collective-permute-done((bf16[512,256]{1,0:T(8,128)(2,1)S(1)}, bf16[512,256]{1,0:T(8,128)(2,1)S(1)}, u32[]{:S(2)}, u32[]{:S(2)}) %collective-permute-start.2) | collective-permute-done | bytes 262176 | tf_op jit(solution)/shard_map/ppermute | solution.py:309
  82.3 1.3 %maximum_convert_fusion = f32[3,512,256]{2,1,0:T(8,128)} fusion(bf16[1,512,256]{2,1,0:T(8,128)(2,1)S(1)} %select_bitcast_fusion, bf16[1,512,256]{2,1,0:T(8,128)(2,1)S(1)} %select_bitcast_fusion.1, bf16[1,512,256]{2,1,0:T(8,128)(2,1)S(1)} %select_bitcast_fusion.2), kind=kLoop, calls=%fused_computation | loop fusion | flops 1179648 | bytes 2359296 | tf_op jit(solution)/shard_map/stack | solution.py:339
  (9 shorter events, 0.1 us)
Async XLA Ops:
  8.3 15.1 %copy-start.7 = (bf16[128,256]{1,0:T(8,128)(2,1)S(1)}, bf16[128,256]{1,0:T(8,128)(2,1)}, u32[]{:S(2)}) copy-start(bf16[128,256]{1,0:T(8,128)(2,1)} %cot_ref.1) | copy-start | bytes 196612
  8.3 15.1 %copy-start.8 = (f32[3,256]{1,0:T(4,128)S(1)}, f32[3,256]{1,0:T(4,128)}, u32[]{:S(2)}) copy-start(f32[3,256]{1,0:T(4,128)} %gain_ref.1) | copy-start | bytes 9220
  8.3 15.1 %copy-start.9 = (s32[128]{0:T(128)S(1)}, s32[128]{0:T(128)}, u32[]{:S(2)}) copy-start(s32[128]{0:T(128)} %param.13) | copy-start | bytes 1540
  8.3 15.1 %all-to-all-start = ((bf16[8,128,256]{2,1,0:T(8,128)(2,1)}), bf16[8,128,256]{2,1,0:T(8,128)(2,1)S(1)}, u32[]{:S(2)}, u32[]{:S(2)}) async-start(bf16[8,128,256]{2,1,0:T(8,128)(2,1)} %bitcast.13), calls=%async_computation | async-start | bytes 1048576 | tf_op jit(solution)/shard_map/all_to_all | solution.py:331
  13.6 1.2 %copy-start = (bf16[1024,512]{1,0:T(8,128)(2,1)S(1)}, bf16[1024,512]{1,0:T(8,128)(2,1)}, u32[]{:S(2)}) copy-start(bf16[1024,512]{1,0:T(8,128)(2,1)} %x_ref.1) | copy-start | bytes 3145732
  14.9 0.9 %copy-start.6 = (f32[3,8,1024]{2,1,0:T(8,128)S(1)}, f32[3,8,1024]{2,1,0:T(8,128)}, u32[]{:S(2)}) copy-start(f32[3,8,1024]{2,1,0:T(8,128)} %get-tuple-element.21.inv_ref) | copy-start | bytes 294916
  16.6 16.4 %copy-start.4 = (f32[1024,128]{1,0:T(8,128)}, f32[1024,128]{1,0:T(8,128)S(1)}, u32[]{:S(2)}) copy-start(f32[1024,128]{1,0:T(8,128)S(1)} %get-tuple-element.33.col_ref) | copy-start | bytes 1572868
  33.1 1.6 %copy-start.3 = (bf16[1024,1024]{1,0:T(8,128)(2,1)S(1)}, bf16[1024,1024]{1,0:T(8,128)(2,1)}, u32[]{:S(2)}) copy-start(bf16[1024,1024]{1,0:T(8,128)(2,1)} %get-tuple-element.32.adj_ref) | copy-start | bytes 6291460
  34.7 1.0 %copy-start.5 = (f32[1024,128]{1,0:T(8,128)S(1)}, f32[1024,128]{1,0:T(8,128)}, u32[]{:S(2)}) copy-start(f32[1024,128]{1,0:T(8,128)} %copy-done.4) | copy-start | bytes 1572868
  37.1 11.3 %collective-permute-start.6 = (bf16[512,256]{1,0:T(8,128)(2,1)S(1)}, bf16[512,256]{1,0:T(8,128)(2,1)}, u32[]{:S(2)}, u32[]{:S(2)}) collective-permute-start(bf16[512,256]{1,0:T(8,128)(2,1)S(1)} %get-tuple-element.35), channel_id=1, source_target_pairs={{0,8},{24,16},{1,9},{25,17},{2,10},{26,18},{3,11},{27,19},{4,12},{... | collective-permute-start | bytes 786440 | tf_op jit(solution)/shard_map/ppermute | solution.py:302
  41.3 1.6 %copy-start.2 = (bf16[1024,1024]{1,0:T(8,128)(2,1)S(1)}, bf16[1024,1024]{1,0:T(8,128)(2,1)}, u32[]{:S(2)}) copy-start(bf16[1024,1024]{1,0:T(8,128)(2,1)} %get-tuple-element.28.adj_ref) | copy-start | bytes 6291460
  42.9 2.7 %copy-start.1 = (bf16[1024,1024]{1,0:T(8,128)(2,1)S(1)}, bf16[1024,1024]{1,0:T(8,128)(2,1)}, u32[]{:S(2)}) copy-start(bf16[1024,1024]{1,0:T(8,128)(2,1)} %get-tuple-element.23.adj_ref) | copy-start | bytes 6291460
  44.3 8.5 %collective-permute-start.3 = (bf16[512,256]{1,0:T(8,128)(2,1)S(1)}, bf16[512,256]{1,0:T(8,128)(2,1)S(1)}, u32[]{:S(2)}, u32[]{:S(2)}) collective-permute-start(bf16[512,256]{1,0:T(8,128)(2,1)S(1)} %get-tuple-element.31), channel_id=1, source_target_pairs={{0,8},{24,16},{1,9},{25,17},{2,10},{26,18},{3,11},{27,19},{4,12},{... | collective-permute-start | bytes 786440 | tf_op jit(solution)/shard_map/ppermute | solution.py:302
  47.1 10.8 %collective-permute-start = (bf16[512,256]{1,0:T(8,128)(2,1)S(1)}, bf16[512,256]{1,0:T(8,128)(2,1)S(1)}, u32[]{:S(2)}, u32[]{:S(2)}) collective-permute-start(bf16[512,256]{1,0:T(8,128)(2,1)S(1)} %get-tuple-element.27), channel_id=1, source_target_pairs={{0,8},{24,16},{1,9},{25,17},{2,10},{26,18},{3,11},{27,19},{4,12},{... | collective-permute-start | bytes 786440 | tf_op jit(solution)/shard_map/ppermute | solution.py:302
  49.4 9.2 %collective-permute-start.7 = (bf16[512,256]{1,0:T(8,128)(2,1)S(1)}, bf16[512,256]{1,0:T(8,128)(2,1)S(1)}, u32[]{:S(2)}, u32[]{:S(2)}) collective-permute-start(bf16[512,256]{1,0:T(8,128)(2,1)S(1)} %reduce-precision_convert_fusion.1), channel_id=1, source_target_pairs={{8,16},{16,8},{9,17},{17,9},{10,18},{18,10},{11,19},{19,11},{12,20... | collective-permute-start | bytes 786440 | tf_op jit(solution)/shard_map/ppermute | solution.py:304
  52.9 7.1 %collective-permute-start.4 = (bf16[512,256]{1,0:T(8,128)(2,1)S(1)}, bf16[512,256]{1,0:T(8,128)(2,1)S(1)}, u32[]{:S(2)}, u32[]{:S(2)}) collective-permute-start(bf16[512,256]{1,0:T(8,128)(2,1)S(1)} %reduce-precision_convert_fusion.3), channel_id=1, source_target_pairs={{8,16},{16,8},{9,17},{17,9},{10,18},{18,10},{11,19},{19,11},{12,20... | collective-permute-start | bytes 786440 | tf_op jit(solution)/shard_map/ppermute | solution.py:304
  58.0 3.5 %collective-permute-start.1 = (bf16[512,256]{1,0:T(8,128)(2,1)S(1)}, bf16[512,256]{1,0:T(8,128)(2,1)S(1)}, u32[]{:S(2)}, u32[]{:S(2)}) collective-permute-start(bf16[512,256]{1,0:T(8,128)(2,1)S(1)} %reduce-precision_convert_fusion.5), channel_id=1, source_target_pairs={{8,16},{16,8},{9,17},{17,9},{10,18},{18,10},{11,19},{19,11},{12,20... | collective-permute-start | bytes 786440 | tf_op jit(solution)/shard_map/ppermute | solution.py:304
  58.7 13.8 %collective-permute-start.8 = (bf16[512,256]{1,0:T(8,128)(2,1)S(1)}, bf16[512,256]{1,0:T(8,128)(2,1)S(1)}, u32[]{:S(2)}, u32[]{:S(2)}) collective-permute-start(bf16[512,256]{1,0:T(8,128)(2,1)S(1)} %reduce-precision_convert_fusion), channel_id=1, source_target_pairs={{8,0},{16,24},{9,1},{17,25},{10,2},{18,26},{11,3},{19,27},{12,4},{... | collective-permute-start | bytes 786440 | tf_op jit(solution)/shard_map/ppermute | solution.py:309
  60.1 18.0 %collective-permute-start.5 = (bf16[512,256]{1,0:T(8,128)(2,1)S(1)}, bf16[512,256]{1,0:T(8,128)(2,1)S(1)}, u32[]{:S(2)}, u32[]{:S(2)}) collective-permute-start(bf16[512,256]{1,0:T(8,128)(2,1)S(1)} %reduce-precision_convert_fusion.2), channel_id=1, source_target_pairs={{8,0},{16,24},{9,1},{17,25},{10,2},{18,26},{11,3},{19,27},{12,4},{... | collective-permute-start | bytes 786440 | tf_op jit(solution)/shard_map/ppermute | solution.py:309
  61.5 20.8 %collective-permute-start.2 = (bf16[512,256]{1,0:T(8,128)(2,1)S(1)}, bf16[512,256]{1,0:T(8,128)(2,1)S(1)}, u32[]{:S(2)}, u32[]{:S(2)}) collective-permute-start(bf16[512,256]{1,0:T(8,128)(2,1)S(1)} %reduce-precision_convert_fusion.4), channel_id=1, source_target_pairs={{8,0},{16,24},{9,1},{17,25},{10,2},{18,26},{11,3},{19,27},{12,4},{... | collective-permute-start | bytes 786440 | tf_op jit(solution)/shard_map/ppermute | solution.py:309
where the time goes:
time: 84.2 us; the launch traced here: 83.6 us
  waiting for transfers between devices  33.2 us (39%)
  starting transfers between devices  18 us (21%)
  Pallas kernels  13.6 us (16%)
  blocking collectives  8.9 us (11%)
  local copies, waits for them, and re-layouts  6.36 us (8%)
  other arithmetic  2.68 us (3%)
  between operations  0.85 us (1%)
    ppermute x3, waiting for transfers between devices, chain_sum(): got = lax.ppermute(sent, 'dom', [(low, low - 1), (high, high + 1)])  19.4 us
    all_gather x1, blocking collectives, dense_body(): slopes = lax.all_gather(slope, 'feat', axis=0, tiled=True)  8.9 us
    pallas_call x1, Pallas kernels, forward(): pl.pallas_call(forward_kernel, name='forward', out_shape=[jax.ShapeDtypeS...  7.65 us
    ppermute x3, waiting for transfers between devices, chain_sum(): total = rounded(total + lax.ppermute(sent, 'dom', perm).astype(F32))  7.06 us
    ppermute x3, starting transfers between devices, chain_sum(): total = rounded(total + lax.ppermute(sent, 'dom', perm).astype(F32))  6.82 us
    all_to_all x1, waiting for transfers between devices, dense_body(): parts = lax.all_to_all(partial, 'feat', 0, 0, tiled=True)  6.74 us
    unnamed x20, local copies, waits for them, and re-layouts  6.36 us
    all_to_all x1, starting transfers between devices, dense_body(): parts = lax.all_to_all(partial, 'feat', 0, 0, tiled=True)  5.31 us
  transfers between devices with their start and end apart: 10, of which 6 were waited for; matrix products, arithmetic and copies ran while one was open for 2% of the time, Pallas kernels for 4%

commit v1 on v0

v1 whole, which is shorter than its diff:
```python
import functools

import jax
import jax.numpy as jnp
from jax import lax
from jax.experimental import pallas as pl
from jax.experimental.pallas import tpu as pltpu
from jax.sharding import PartitionSpec as P

BLK = 128
MIB = 1024 * 1024
BF16 = jnp.bfloat16
F32 = jnp.float32


def unpack_bits(packed):
    shifts = (2 ** jnp.arange(16)).astype(jnp.int32)
    bit_values = packed[..., None] // shifts % 2
    bit_values = jnp.swapaxes(bit_values, -3, -2)
    return bit_values.reshape(packed.shape[:-2] + (packed.shape[-1], packed.shape[-2] * 16))


def silu_grad(pre_act):
    sigmoid_value = jax.nn.sigmoid(pre_act)
    return sigmoid_value * (1.0 + pre_act * (1.0 - sigmoid_value))


def type_rows(node_type, type_gain):
    onehot = (
        node_type[:, None] == jnp.arange(type_gain.shape[0], dtype=jnp.int32)[None, :]
    ).astype(jnp.float32)
    return jnp.sum(onehot[:, :, None] * type_gain[None, :, :], axis=1)


def aggregate(features, source_block, slot_count, block_pattern):
    count_blocks = source_block.shape[0]
    relations = source_block.shape[1]
    slots_each = source_block.shape[2]
    col_width = features.shape[1]
    blocks = features.reshape(count_blocks, BLK, col_width)
    blocks_wide = blocks.astype(jnp.float32)
    live_slots = (
        jnp.arange(slots_each, dtype=jnp.int32)[None, None, :] < slot_count[:, :, None]
    ).astype(jnp.float32)
    mixed_list = []
    for relation in range(relations):
        summed = jnp.zeros((count_blocks, BLK, col_width), jnp.float32)
        degree = jnp.zeros((count_blocks, BLK), jnp.float32)
        for slot_index in range(slots_each):
            adjacency = (
                unpack_bits(block_pattern[:, relation, slot_index]).astype(jnp.float32)
                * live_slots[:, relation, slot_index][:, None, None]
            )
            picked = jnp.take(blocks, source_block[:, relation, slot_index], axis=0)
            summed = summed + jnp.einsum(
                "bij,bjc->bic",
                adjacency.astype(jnp.bfloat16),
                picked,
                preferred_element_type=jnp.float32,
            )
            degree = degree + jnp.sum(adjacency, axis=2)
        mixed_rows = ((blocks_wide + summed) / (1.0 + degree)[:, :, None]).astype(jnp.bfloat16)
        mixed_list.append(mixed_rows.reshape(count_blocks * BLK, col_width))
    return jnp.stack(mixed_list)


def general_body(
    features, proj_weight, source_block, slot_count, block_pattern, node_type, type_gain, cotangent
):
    mixed_all = aggregate(features, source_block, slot_count, block_pattern)
    pre_act = lax.psum_scatter(
        jnp.einsum("rnc,rch->nh", mixed_all, proj_weight, preferred_element_type=jnp.float32),
        "feat",
        scatter_dimension=0,
        tiled=True,
    )
    row_gains = type_rows(node_type, type_gain)
    output = (jax.nn.silu(pre_act) * row_gains).astype(jnp.bfloat16)
    slope_rows = (cotangent.astype(jnp.float32) * row_gains * silu_grad(pre_act)).astype(
        jnp.bfloat16
    )
    local_grad = jnp.einsum(
        "rnc,nh->rch",
        mixed_all,
        lax.all_gather(slope_rows, "feat", axis=0, tiled=True),
        preferred_element_type=jnp.float32,
    )
    weight_grad = lax.psum(local_grad, "dom")
    return (output, weight_grad)


STRIP = 2 * BLK


def halving_offsets(core):
    first = jnp.where(core == 0, 2, 4)
    return first, 6 - first


def forward_kernel(src_ref, cnt_ref, pat_hbm, x_hbm, w_hbm, inv_ref, keep_ref, send_ref, *rest):
    relations, slots, blocks = src_ref.shape
    strips = blocks // 2
    adj_out = rest[:relations]
    rest = rest[relations:]
    adj_refs = [rest[r * strips : (r + 1) * strips] for r in range(relations)]
    pat_ref, x_ref, w_ref, pre_ref, in_sem, out_sem = rest[relations * strips :]

    loads = [
        pltpu.make_async_copy(pat_hbm, pat_ref, in_sem.at[0]),
        pltpu.make_async_copy(x_hbm, x_ref, in_sem.at[1]),
        pltpu.make_async_copy(w_hbm, w_ref, in_sem.at[2]),
    ]
    for load in loads:
        load.start()

    sub = lax.broadcasted_iota(jnp.int32, (BLK, BLK), 0)
    lane = lax.broadcasted_iota(jnp.int32, (BLK, BLK), 1)
    eye = jnp.where(sub == lane, 1.0, 0.0).astype(BF16)
    bit = jnp.left_shift(1, lax.broadcasted_iota(jnp.int32, (16, BLK), 0))

    for strip_refs in adj_refs:
        for i, strip in enumerate(strip_refs):
            strip[...] = jnp.zeros(strip.shape, BF16)
            for b in (2 * i, 2 * i + 1):
                lanes = slice((b % 2) * BLK, (b % 2 + 1) * BLK)
                strip[b * BLK : (b + 1) * BLK, lanes] = eye
    loads[0].wait()

    def build(relation):
        degree = [jnp.zeros((8, BLK), jnp.int32)] * blocks
        for s in range(slots):
            for b in range(blocks):
                strip = adj_refs[relation][b // 2]
                lanes = slice((b % 2) * BLK, (b % 2 + 1) * BLK)
                live = jnp.where(s < cnt_ref[relation, b], 0xFFFF, 0)
                words = pat_ref[b, relation, s] & live
                row0 = pl.multiple_of(src_ref[relation, s, b] * BLK, BLK)
                parts = [
                    jnp.where((words[w : w + 1, :] & bit) != 0, 1.0, 0.0)
                    for w in range(words.shape[0])
                ]
                tile = jnp.concatenate(parts, axis=0).astype(BF16)
                strip[pl.ds(row0, BLK), lanes] += tile
                c = words - ((words >> 1) & 0x5555)
                c = (c & 0x3333) + ((c >> 2) & 0x3333)
                c = (c + (c >> 4)) & 0x0F0F
                degree[b] = degree[b] + ((c + (c >> 8)) & 0x1F)
        for b in range(blocks):
            total = jnp.sum(degree[b].astype(F32), axis=0, keepdims=True)
            inv_ref[relation, 0:1, b * BLK : (b + 1) * BLK] = 1.0 / (1.0 + total)

    stores = []
    for relation in range(relations):
        build(relation)
        for i, strip in enumerate(adj_refs[relation]):
            store = pltpu.make_async_copy(
                strip,
                adj_out[relation].at[:, pl.ds(i * STRIP, STRIP)],
                out_sem.at[relation * strips + i],
            )
            store.start()
            stores.append(store)
        if relation == 0:
            loads[1].wait()
            loads[2].wait()
        w_t = w_ref[relation].T
        y_t = lax.dot_general(
            w_t, x_ref[...], (((1,), (1,)), ((), ())), preferred_element_type=F32
        ).astype(BF16)
        for i, strip in enumerate(adj_refs[relation]):
            lanes = slice(i * STRIP, (i + 1) * STRIP)
            p_t = jnp.dot(y_t, strip[...], preferred_element_type=F32)
            p_t = p_t * inv_ref[relation, 0:1, lanes]
            if relation == 0:
                pre_ref[:, lanes] = p_t
            else:
                pre_ref[:, lanes] += p_t

    me = lax.axis_index("feat")
    one, two = halving_offsets(me % 2)

    def block(k):
        return pre_ref[:, pl.ds(pl.multiple_of((me ^ k) * BLK, BLK), BLK)].T

    for i, k in enumerate((1, 1 ^ one, 1 ^ two, 7)):
        send_ref[i * BLK : (i + 1) * BLK, :] = block(k).astype(BF16)
    for i, k in enumerate((0, two, one, 6)):
        keep_ref[i * BLK : (i + 1) * BLK, :] = block(k)
    for store in stores:
        store.wait()


def forward(features, proj_weight, source_block, slot_count, block_pattern):
    nodes, cols = features.shape
    relations, _, hidden = proj_weight.shape
    strips = nodes // STRIP
    hbm = pl.BlockSpec(memory_space=pltpu.HBM)
    smem = pl.BlockSpec(memory_space=pltpu.SMEM)
    vmem = pl.BlockSpec(memory_space=pltpu.VMEM)
    inv_deg, keep, send, *adj = pl.pallas_call(
        forward_kernel,
        name="forward",
        out_shape=[
            jax.ShapeDtypeStruct((relations, 8, nodes), F32),
            jax.ShapeDtypeStruct((nodes // 2, hidden), F32),
            jax.ShapeDtypeStruct((nodes // 2, hidden), BF16),
        ]
        + [jax.ShapeDtypeStruct((nodes, nodes), BF16)] * relations,
        in_specs=[smem, smem, hbm, hbm, hbm],
        out_specs=[vmem] * 3 + [hbm] * relations,
        scratch_shapes=[pltpu.VMEM((nodes, STRIP), BF16)] * (relations * strips)
        + [
            pltpu.VMEM(block_pattern.shape, jnp.int32),
            pltpu.VMEM(features.shape, BF16),
            pltpu.VMEM(proj_weight.shape, BF16),
            pltpu.VMEM((hidden, nodes), F32),
            pltpu.SemaphoreType.DMA((3,)),
            pltpu.SemaphoreType.DMA((relations * strips,)),
        ],
        compiler_params=pltpu.CompilerParams(vmem_limit_bytes=64 * MIB),
    )(
        jnp.transpose(source_block, (1, 2, 0)),
        jnp.transpose(slot_count, (1, 0)),
        block_pattern,
        features,
        proj_weight,
    )
    return inv_deg, keep, send, adj


def halve(keep, send):
    def swap(value, step):
        def partner(f):
            order = (2, 4) if f % 2 == 0 else (4, 2)
            return f ^ (1, order[0], order[1])[step]

        return lax.ppermute(value, "feat", [(f, partner(f)) for f in range(8)])

    got1 = swap(send, 0)
    half, rows = keep.shape[0] // 2, keep.shape[0] // 4
    sent2 = (keep[half:] + got1[half:].astype(F32)).astype(BF16)
    got2 = swap(sent2, 1)
    sent3 = keep[rows:half] + got1[rows:half].astype(F32) + got2[rows:].astype(F32)
    got3 = swap(sent3.astype(BF16), 2)
    return keep, got1, got2, got3


def combine_kernel(
    keep_ref, got1_ref, got2_ref, got3_ref, type_ref, gain_ref, cot_ref, act_ref, slope_ref
):
    rows = act_ref.shape[0]
    pre = keep_ref[...] + got1_ref[...].astype(F32)
    pre = pre + got2_ref[...].astype(F32) + got3_ref[...].astype(F32)
    types = jnp.broadcast_to(type_ref[...].astype(F32), (rows, rows)).T
    types = jnp.concatenate([types] * (act_ref.shape[1] // rows), axis=1)
    gain = jnp.zeros(act_ref.shape, F32)
    for t in range(gain_ref.shape[0]):
        gain = jnp.where(types == t, gain_ref[t : t + 1, :], gain)
    sig = jax.nn.sigmoid(pre)
    act_ref[...] = (pre * sig * gain).astype(BF16)
    grad = sig * (1.0 + pre * (1.0 - sig))
    slope_ref[...] = (cot_ref[...].astype(F32) * gain * grad).astype(BF16)


def combine(parts, node_type, type_gain, cotangent):
    shape = cotangent.shape
    first = pl.BlockSpec(shape, lambda i: (0, 0))
    return pl.pallas_call(
        combine_kernel,
        name="combine",
        grid=(1,),
        out_shape=[jax.ShapeDtypeStruct(shape, BF16)] * 2,
        in_specs=[first] * 4
        + [
            pl.BlockSpec((1, shape[0]), lambda i: (0, 0)),
            pl.BlockSpec(type_gain.shape, lambda i: (0, 0)),
            first,
        ],
        out_specs=[first] * 2,
        compiler_params=pltpu.CompilerParams(vmem_limit_bytes=6 * MIB),
    )(*parts, node_type[None, :], type_gain, cotangent)


def gradient_kernel(
    relation, x_hbm, adj_hbm, inv_hbm, slope_hbm, wide_ref, sent_ref,
    x_ref, adj_ref, inv_ref, slope_ref, scaled_ref, sem,
):
    nodes = x_ref.shape[0]
    step = nodes // 4
    loads = [
        pltpu.make_async_copy(inv_hbm.at[relation], inv_ref, sem.at[0]),
        pltpu.make_async_copy(slope_hbm, slope_ref, sem.at[1]),
    ]
    for i in range(4):
        rows = pl.ds(i * step, step)
        loads.append(pltpu.make_async_copy(adj_hbm.at[rows], adj_ref.at[rows], sem.at[2 + 2 * i]))
        loads.append(pltpu.make_async_copy(x_hbm.at[rows], x_ref.at[rows], sem.at[3 + 2 * i]))
    for load in loads:
        load.start()
    loads[0].wait()
    loads[1].wait()
    for b in range(nodes // BLK):
        rows = slice(b * BLK, (b + 1) * BLK)
        inv = jnp.broadcast_to(inv_ref[0:1, rows], (BLK, BLK)).T
        inv = jnp.concatenate([inv] * (slope_ref.shape[1] // BLK), axis=1)
        scaled_ref[rows, :] = (slope_ref[rows, :].astype(F32) * inv).astype(BF16)
    grad = None
    for i in range(4):
        rows = slice(i * step, (i + 1) * step)
        loads[2 + 2 * i].wait()
        loads[3 + 2 * i].wait()
        spread = jnp.dot(adj_ref[rows, :], scaled_ref[...], preferred_element_type=F32)
        part = jnp.dot(x_ref[rows, :].T, spread.astype(BF16), preferred_element_type=F32)
        grad = part if grad is None else grad + part
    wide_ref[...] = grad
    sent_ref[...] = grad.astype(BF16)


def gradient(relation, features, adj, inv_deg, slopes):
    nodes, cols = features.shape
    hidden = slopes.shape[1]
    hbm = pl.BlockSpec(memory_space=pltpu.HBM)
    vmem = pl.BlockSpec(memory_space=pltpu.VMEM)
    return pl.pallas_call(
        functools.partial(gradient_kernel, relation),
        name="gradient",
        out_shape=[
            jax.ShapeDtypeStruct((cols, hidden), F32),
            jax.ShapeDtypeStruct((cols, hidden), BF16),
        ],
        in_specs=[hbm] * 4,
        out_specs=[vmem] * 2,
        scratch_shapes=[
            pltpu.VMEM((nodes, cols), BF16),
            pltpu.VMEM((nodes, nodes), BF16),
            pltpu.VMEM((8, nodes), F32),
            pltpu.VMEM((nodes, hidden), BF16),
            pltpu.VMEM((nodes, hidden), BF16),
            pltpu.SemaphoreType.DMA((10,)),
        ],
        compiler_params=pltpu.CompilerParams(vmem_limit_bytes=64 * MIB),
        cost_estimate=pl.CostEstimate(
            flops=2 * nodes * hidden * (nodes + cols),
            bytes_accessed=2 * nodes * nodes + 6 * cols * hidden,
            transcendentals=0,
        ),
    )(features, adj, inv_deg, slopes)


def rounded(x):
    return lax.reduce_precision(x, 8, 7)


def chain_sum(chunks, n_dom):
    half = n_dom // 2
    at = lax.axis_index("dom")
    inner = []
    for wide, sent in chunks:
        for hop in range(half - 1):
            perm = [(hop, hop + 1), (n_dom - 1 - hop, n_dom - 2 - hop)]
            wide = rounded(wide + lax.ppermute(sent, "dom", perm).astype(F32))
            sent = wide.astype(BF16)
        inner.append(sent)
    middle = []
    for i, sent in enumerate(inner):
        if i >= 2:
            sent, _ = lax.optimization_barrier((sent, middle[i - 2]))
        got = lax.ppermute(sent, "dom", [(half - 1, half), (half, half - 1)])
        middle.append(rounded(sent.astype(F32) + got.astype(F32)).astype(BF16))
    outer = []
    for i, sent in enumerate(middle):
        if i >= 2:
            sent, outer[i - 2] = lax.optimization_barrier((sent, outer[i - 2]))
        for hop in range(half - 1):
            low, high = half - 1 - hop, half + hop
            got = lax.ppermute(sent, "dom", [(low, low - 1), (high, high + 1)])
            sent = jnp.where((at < low) | (at > high), got, sent)
        outer.append(sent)
    return [sent.astype(F32) for sent in outer]


def dense_body(
    n_dom,
    features,
    proj_weight,
    source_block,
    slot_count,
    block_pattern,
    node_type,
    type_gain,
    cotangent,
):
    inv_deg, keep, send, adj = forward(
        features, proj_weight, source_block, slot_count, block_pattern
    )
    parts = halve(keep, send)
    activations, slope = combine(parts, node_type, type_gain, cotangent)
    slopes = lax.all_gather(slope, "feat", axis=0, tiled=True)
    chunks = [
        gradient(relation, features, adj[relation], inv_deg, slopes)
        for relation in range(proj_weight.shape[0])
    ]
    return activations, jnp.stack(chain_sum(chunks, n_dom))


def body(n_dom, n_feat, *args):
    nodes, relations = args[0].shape[0], args[2].shape[1]
    fits = 2 * relations * nodes * nodes <= 8 * MIB
    if fits and n_feat == 8 and n_dom % 2 == 0 and nodes == n_feat * BLK:
        return dense_body(n_dom, *args)
    return general_body(*args)


def solution(mesh):
    placed = (
        P("dom", "feat"),
        P(None, "feat", None),
        P("dom", None, None),
        P("dom", None),
        P("dom", None, None, None, None),
        P(("dom", "feat")),
        P(),
        P(("dom", "feat"), None),
    )
    return jax.shard_map(
        functools.partial(body, mesh.shape["dom"], mesh.shape["feat"]),
        mesh=mesh,
        in_specs=placed,
        out_specs=(P(("dom", "feat"), None), P(None, "feat", None)),
        check_vma=False,
    )
```

time: 84.2 us -> 93.4 us (1.11)
  Pallas kernels: 13.6 us -> 23.1 us
  waiting for transfers between devices: 33.2 us -> 29.3 us
  other arithmetic: 2.68 us -> 5.86 us
  local copies, waits for them, and re-layouts: 6.36 us -> 3.23 us
  blocking collectives: 8.9 us -> 11.4 us
  starting transfers between devices: 18 us -> 19.1 us
    pallas_call x5 -> x4, Pallas kernels: 5.91 us -> 14.5 us  [the longest x3 13.8 us: gradient(): pl.pallas_call(functools.partial(gradient_kernel, relation), name='gradie...]
    all_to_all x1 -> x0, waiting for transfers between devices: 6.74 us -> none  [dense_body(): parts = lax.all_to_all(partial, 'feat', 0, 0, tiled=True)]
    ppermute x3 -> x6, starting transfers between devices: 6.82 us -> 13.2 us  [the longest x3 7.63 us: chain_sum(): wide = rounded(wide + lax.ppermute(sent, 'dom', perm).astype(F32))]
    all_to_all x1 -> x0, starting transfers between devices: 5.31 us -> none  [dense_body(): parts = lax.all_to_all(partial, 'feat', 0, 0, tiled=True)]
    convert_element_type x6 -> x8, other arithmetic: 1.32 us -> 4.5 us  [the longest x3 2.4 us: chain_sum(): sent = wide.astype(BF16)]
    unnamed x20 -> x10, local copies, waits for them, and re-layouts: 6.36 us -> 3.23 us
    all_gather x1, blocking collectives: 8.9 us -> 11.4 us  [dense_body(): slopes = lax.all_gather(slope, 'feat', axis=0, tiled=True)]
    ppermute x3 -> x6, waiting for transfers between devices: 7.06 us -> 9.2 us  [the longest x3 6.57 us: swap(): return lax.ppermute(value, 'feat', [(f, partner(f)) for f in range(8)])]
  transfers between devices with their start and end apart: 10 -> 12, of which waited for: 6 -> 7; matrix products, arithmetic and copies ran while one was open for 2% -> 3% of each run, Pallas kernels for 4% -> 10%
where the time goes in v1:
time: 93.4 us; the launch traced here: 92.8 us
  waiting for transfers between devices  29.3 us (31%)
  Pallas kernels  23.1 us (25%)
  starting transfers between devices  19.1 us (20%)
  blocking collectives  11.4 us (12%)
  other arithmetic  5.86 us (6%)
  local copies, waits for them, and re-layouts  3.23 us (3%)
    ppermute x3, waiting for transfers between devices, chain_sum(): got = lax.ppermute(sent, 'dom', [(low, low - 1), (high, high + 1)])  20.1 us
    pallas_call x3, Pallas kernels, gradient(): pl.pallas_call(functools.partial(gradient_kernel, relation), name='gradie...  13.8 us
    all_gather x1, blocking collectives, dense_body(): slopes = lax.all_gather(slope, 'feat', axis=0, tiled=True)  11.4 us
    pallas_call x1, Pallas kernels, forward(): pl.pallas_call(forward_kernel, name='forward', out_shape=[jax.ShapeDtypeS...  8.6 us
    ppermute x3, starting transfers between devices, chain_sum(): wide = rounded(wide + lax.ppermute(sent, 'dom', perm).astype(F32))  7.63 us
    ppermute x3, waiting for transfers between devices, swap(): return lax.ppermute(value, 'feat', [(f, partner(f)) for f in range(8)])  6.57 us
    ppermute x3, starting transfers between devices, swap(): return lax.ppermute(value, 'feat', [(f, partner(f)) for f in range(8)])  5.56 us
    ppermute x3, starting transfers between devices, chain_sum(): got = lax.ppermute(sent, 'dom', [(low, low - 1), (high, high + 1)])  3.88 us
  transfers between devices with their start and end apart: 12, of which 7 were waited for; matrix products, arithmetic and copies ran while one was open for 3% of the time, Pallas kernels for 10%

profile of v1, /device:TPU:0, one launch (start us, length us, event | category | flops | bytes accessed | tf_op | source)
XLA Modules:
  0.0 92.8 jit_solution(8703789221079185148)
XLA Ops:
  0.6 8.6 %forward.1 = (f32[3,8,1024]{2,1,0:T(8,128)}, f32[512,256]{1,0:T(8,128)}, bf16[512,256]{1,0:T(8,128)(2,1)}, bf16[1024,1024]{1,0:T(8,128)(2,1)}, bf16[1024,1024]{1,0:T(8,128)(2,1)}, /*index=5*/bf16[1024,1024]{1,0:T(8,128)(2,1)}) custom-call(s32[3,4,8]{2,1,0:T(4,128)} %bitcast.10, s32[3,8]{1,0:T(4,128)} %bitcast.11, s32[8,3,4,8,128]{4,3,2,1,0:T(8,128)} %pat_hbm.1, ...), custom_call_target="tpu_custom_call" | custom-call | tf_op jit(solution)/shard_map/forward/pallas_call | solution.py:200
  9.2 0.5 collective-permute-start
  9.8 1.4 %collective-permute-done.got1_ref = bf16[512,256]{1,0:T(8,128)(2,1)S(1)} collective-permute-done((bf16[512,256]{1,0:T(8,128)(2,1)}, bf16[512,256]{1,0:T(8,128)(2,1)S(1)}, u32[]{:S(2)}, u32[]{:S(2)}) %collective-permute-start) | collective-permute-done | bytes 262176 | tf_op jit(solution)/shard_map/ppermute | solution.py:237
  11.1 1.0 %add_convert_fusion = bf16[256,256]{1,0:T(8,128)(2,1)S(1)} fusion(f32[512,256]{1,0:T(8,128)} %get-tuple-element.19.keep_ref, bf16[512,256]{1,0:T(8,128)(2,1)S(1)} %collective-permute-done.got1_ref), kind=kLoop, calls=%fused_computation.9 | loop fusion | flops 196608 | bytes 524288 | tf_op jit(solution)/shard_map/convert_element_type | solution.py:241
  12.1 2.9 %collective-permute-start.1 = (bf16[256,256]{1,0:T(8,128)(2,1)S(1)}, bf16[256,256]{1,0:T(8,128)(2,1)S(1)}, u32[]{:S(2)}, u32[]{:S(2)}) collective-permute-start(bf16[256,256]{1,0:T(8,128)(2,1)S(1)} %add_convert_fusion), channel_id=1, source_target_pairs={{0,2},{1,5},{2,0},{3,7},{4,6},{5,1},{6,4},{7,3},{8,10},{9,13},{10,... | collective-permute-start | bytes 393224 | tf_op jit(solution)/shard_map/ppermute | solution.py:237
  15.0 2.9 %collective-permute-done.1.got2_ref = bf16[256,256]{1,0:T(8,128)(2,1)S(1)} collective-permute-done((bf16[256,256]{1,0:T(8,128)(2,1)S(1)}, bf16[256,256]{1,0:T(8,128)(2,1)S(1)}, u32[]{:S(2)}, u32[]{:S(2)}) %collective-permute-start.1) | collective-permute-done | bytes 131104 | tf_op jit(solution)/shard_map/ppermute | solution.py:237
  18.0 0.9 %add_convert_fusion.1 = bf16[128,256]{1,0:T(8,128)(2,1)S(1)} fusion(f32[512,256]{1,0:T(8,128)} %get-tuple-element.19.keep_ref, bf16[256,256]{1,0:T(8,128)(2,1)S(1)} %collective-permute-done.1.got2_ref, bf16[512,256]{1,0:T(8,128)(2,1)S(1)} %collective-permute-done.got1_ref), kind=kLoop, calls=%fused_computation.11 | loop fusion | flops 163840 | bytes 327680 | tf_op jit(solution)/shard_map/convert_element_type | solution.py:244
  18.9 2.1 %collective-permute-start.2 = (bf16[128,256]{1,0:T(8,128)(2,1)S(1)}, bf16[128,256]{1,0:T(8,128)(2,1)S(1)}, u32[]{:S(2)}, u32[]{:S(2)}) collective-permute-start(bf16[128,256]{1,0:T(8,128)(2,1)S(1)} %add_convert_fusion.1), channel_id=1, source_target_pairs={{0,4},{1,3},{2,6},{3,1},{4,0},{5,7},{6,2},{7,5},{8,12},{9,11},{10,... | collective-permute-start | bytes 196616 | tf_op jit(solution)/shard_map/ppermute | solution.py:237
  21.0 2.2 %collective-permute-done.2.got3_ref = bf16[128,256]{1,0:T(8,128)(2,1)S(1)} collective-permute-done((bf16[128,256]{1,0:T(8,128)(2,1)S(1)}, bf16[128,256]{1,0:T(8,128)(2,1)S(1)}, u32[]{:S(2)}, u32[]{:S(2)}) %collective-permute-start.2) | collective-permute-done | bytes 65568 | tf_op jit(solution)/shard_map/ppermute | solution.py:237
  23.3 0.0 copy-start
  23.3 1.0 %copy-done = f32[512,256]{1,0:T(8,128)S(1)} copy-done((f32[512,256]{1,0:T(8,128)S(1)}, f32[512,256]{1,0:T(8,128)}, u32[]{:S(2)}) %copy-start) | copy-done | bytes 524312
  24.3 0.0 copy-start.1
  24.3 0.8 copy-done.1
  25.2 0.0 copy-start.2
  25.2 0.7 copy-done.2
  25.9 0.7 copy-done.3
  26.5 0.7 combine.1
  27.3 11.4 %all_gather.3.slope_hbm = bf16[1024,256]{1,0:T(8,128)(2,1)} all-gather(bf16[128,256]{1,0:T(8,128)(2,1)S(1)} %get-tuple-element.24), channel_id=1, replica_groups=mesh['dom'=4,'feat'=8] {'feat'}, dimensions={0}, use_global_device_ids=true | all-gather | bytes 589824 | tf_op jit(solution)/shard_map/all_gather | solution.py:398
  38.7 4.6 %gradient.4 = (f32[512,256]{1,0:T(8,128)}, bf16[512,256]{1,0:T(8,128)(2,1)}) custom-call(bf16[1024,512]{1,0:T(8,128)(2,1)} %x_hbm.7, bf16[1024,1024]{1,0:T(8,128)(2,1)} %get-tuple-element.27.adj_hbm, f32[3,8,1024]{2,1,0:T(8,128)} %get-tuple-element.23.inv_hbm, bf16[1024,256]{1,0:T(8,128)(2,1)} %all_gather.3.slope_hbm), custom_call_target="tpu_custom_call" | custom-call | flops 805306368 | bytes 2883584 | tf_op jit(solution)/shard_map/gradient/pallas_call | solution.py:324
  43.2 4.2 %collective-permute-start.4 = (bf16[512,256]{1,0:T(8,128)(2,1)}, bf16[512,256]{1,0:T(8,128)(2,1)}, u32[]{:S(2)}, u32[]{:S(2)}) collective-permute-start(bf16[512,256]{1,0:T(8,128)(2,1)} %get-tuple-element.29), channel_id=1, source_target_pairs={{0,8},{24,16},{1,9},{25,17},{2,10},{26,18},{3,11},{27,19},{4,12},{... | collective-permute-start | bytes 786440 | tf_op jit(solution)/shard_map/ppermute | solution.py:361
  47.4 4.6 %gradient.5 = (f32[512,256]{1,0:T(8,128)}, bf16[512,256]{1,0:T(8,128)(2,1)}) custom-call(bf16[1024,512]{1,0:T(8,128)(2,1)} %x_hbm.7, bf16[1024,1024]{1,0:T(8,128)(2,1)} %get-tuple-element.32.adj_hbm, f32[3,8,1024]{2,1,0:T(8,128)} %get-tuple-element.23.inv_hbm, bf16[1024,256]{1,0:T(8,128)(2,1)} %all_gather.3.slope_hbm), custom_call_target="tpu_custom_call" | custom-call | flops 805306368 | bytes 2883584 | tf_op jit(solution)/shard_map/gradient/pallas_call | solution.py:324
  52.0 2.0 %collective-permute-start.8 = (bf16[512,256]{1,0:T(8,128)(2,1)}, bf16[512,256]{1,0:T(8,128)(2,1)}, u32[]{:S(2)}, u32[]{:S(2)}) collective-permute-start(bf16[512,256]{1,0:T(8,128)(2,1)} %get-tuple-element.34), channel_id=1, source_target_pairs={{0,8},{24,16},{1,9},{25,17},{2,10},{26,18},{3,11},{27,19},{4,12},{... | collective-permute-start | bytes 786440 | tf_op jit(solution)/shard_map/ppermute | solution.py:361
  54.0 4.6 %gradient.3 = (f32[512,256]{1,0:T(8,128)}, bf16[512,256]{1,0:T(8,128)(2,1)}) custom-call(bf16[1024,512]{1,0:T(8,128)(2,1)} %x_hbm.7, bf16[1024,1024]{1,0:T(8,128)(2,1)} %get-tuple-element.22.adj_hbm, f32[3,8,1024]{2,1,0:T(8,128)} %get-tuple-element.23.inv_hbm, bf16[1024,256]{1,0:T(8,128)(2,1)} %all_gather.3.slope_hbm), custom_call_target="tpu_custom_call" | custom-call | flops 805306368 | bytes 2883584 | tf_op jit(solution)/shard_map/gradient/pallas_call | solution.py:324
  58.6 0.0 copy-start.4
  58.6 1.4 %collective-permute-start.3 = (bf16[512,256]{1,0:T(8,128)(2,1)}, bf16[512,256]{1,0:T(8,128)(2,1)S(1)}, u32[]{:S(2)}, u32[]{:S(2)}) collective-permute-start(bf16[512,256]{1,0:T(8,128)(2,1)} %get-tuple-element.26), channel_id=1, source_target_pairs={{0,8},{24,16},{1,9},{25,17},{2,10},{26,18},{3,11},{27,19},{4,12},{... | collective-permute-start | bytes 786440 | tf_op jit(solution)/shard_map/ppermute | solution.py:361
  60.1 0.0 collective-permute-done.4
  60.1 1.2 %reduce-precision_convert_fusion.4 = bf16[512,256]{1,0:T(8,128)(2,1)S(1)} fusion(f32[512,256]{1,0:T(8,128)} %get-tuple-element.28, bf16[512,256]{1,0:T(8,128)(2,1)} %collective-permute-done.4), kind=kLoop, calls=%fused_computation.5 | loop fusion | flops 524288 | bytes 1048576 | tf_op jit(solution)/shard_map/convert_element_type | solution.py:362
  61.3 0.7 collective-permute-start.5
  61.9 0.0 collective-permute-done.8
  62.0 1.2 %reduce-precision_convert_fusion.1 = bf16[512,256]{1,0:T(8,128)(2,1)S(1)} fusion(f32[512,256]{1,0:T(8,128)} %get-tuple-element.33, bf16[512,256]{1,0:T(8,128)(2,1)} %collective-permute-done.8), kind=kLoop, calls=%fused_computation.2 | loop fusion | flops 524288 | bytes 1048576 | tf_op jit(solution)/shard_map/convert_element_type | solution.py:362
  63.1 0.7 collective-permute-start.9
  63.8 2.6 %collective-permute-done.3 = bf16[512,256]{1,0:T(8,128)(2,1)S(1)} collective-permute-done((bf16[512,256]{1,0:T(8,128)(2,1)}, bf16[512,256]{1,0:T(8,128)(2,1)S(1)}, u32[]{:S(2)}, u32[]{:S(2)}) %collective-permute-start.3) | collective-permute-done | bytes 262176 | tf_op jit(solution)/shard_map/ppermute | solution.py:361
  66.4 0.0 copy-done.4
  66.4 0.1 reduce-precision_convert_fusion.5
  66.5 0.0 collective-permute-done.5
  66.5 0.1 reduce-precision_convert_fusion.3
  66.6 0.7 collective-permute-start.6
  67.3 1.3 %collective-permute-start.7 = (bf16[512,256]{1,0:T(8,128)(2,1)S(1)}, bf16[512,256]{1,0:T(8,128)(2,1)S(1)}, u32[]{:S(2)}, u32[]{:S(2)}) collective-permute-start(bf16[512,256]{1,0:T(8,128)(2,1)S(1)} %reduce-precision_convert_fusion.3), channel_id=1, source_target_pairs={{8,0},{16,24},{9,1},{17,25},{10,2},{18,26},{11,3},{19,27},{12,4},{... | collective-permute-start | bytes 786440 | tf_op jit(solution)/shard_map/ppermute | solution.py:376
  68.6 0.0 collective-permute-done.9
  68.6 0.1 reduce-precision_convert_fusion
  68.7 1.3 %collective-permute-start.10 = (bf16[512,256]{1,0:T(8,128)(2,1)S(1)}, bf16[512,256]{1,0:T(8,128)(2,1)S(1)}, u32[]{:S(2)}, u32[]{:S(2)}) collective-permute-start(bf16[512,256]{1,0:T(8,128)(2,1)S(1)} %reduce-precision_convert_fusion), channel_id=1, source_target_pairs={{8,0},{16,24},{9,1},{17,25},{10,2},{18,26},{11,3},{19,27},{12,4},{... | collective-permute-start | bytes 786440 | tf_op jit(solution)/shard_map/ppermute | solution.py:376
  70.0 0.0 collective-permute-done.6
  70.0 0.1 reduce-precision_convert_fusion.2
  70.1 12.3 %collective-permute-done.7 = bf16[512,256]{1,0:T(8,128)(2,1)S(1)} collective-permute-done((bf16[512,256]{1,0:T(8,128)(2,1)S(1)}, bf16[512,256]{1,0:T(8,128)(2,1)S(1)}, u32[]{:S(2)}, u32[]{:S(2)}) %collective-permute-start.7) | collective-permute-done | bytes 262176 | tf_op jit(solution)/shard_map/ppermute | solution.py:376
  82.4 1.3 %collective-permute-start.11 = (bf16[512,256]{1,0:T(8,128)(2,1)S(1)}, bf16[512,256]{1,0:T(8,128)(2,1)S(1)}, u32[]{:S(2)}, u32[]{:S(2)}) collective-permute-start(bf16[512,256]{1,0:T(8,128)(2,1)S(1)} %reduce-precision_convert_fusion.2), channel_id=1, source_target_pairs={{8,0},{16,24},{9,1},{17,25},{10,2},{18,26},{11,3},{19,27},{12,4},{... | collective-permute-start | bytes 786440 | tf_op jit(solution)/shard_map/ppermute | solution.py:376
  83.7 4.3 %collective-permute-done.10 = bf16[512,256]{1,0:T(8,128)(2,1)S(1)} collective-permute-done((bf16[512,256]{1,0:T(8,128)(2,1)S(1)}, bf16[512,256]{1,0:T(8,128)(2,1)S(1)}, u32[]{:S(2)}, u32[]{:S(2)}) %collective-permute-start.10) | collective-permute-done | bytes 262176 | tf_op jit(solution)/shard_map/ppermute | solution.py:376
  88.0 3.5 %collective-permute-done.11 = bf16[512,256]{1,0:T(8,128)(2,1)S(1)} collective-permute-done((bf16[512,256]{1,0:T(8,128)(2,1)S(1)}, bf16[512,256]{1,0:T(8,128)(2,1)S(1)}, u32[]{:S(2)}, u32[]{:S(2)}) %collective-permute-start.11) | collective-permute-done | bytes 262176 | tf_op jit(solution)/shard_map/ppermute | solution.py:376
  91.5 1.3 %maximum_convert_fusion = f32[3,512,256]{2,1,0:T(8,128)} fusion(bf16[1,512,256]{2,1,0:T(8,128)(2,1)S(1)} %select_bitcast_fusion, bf16[1,512,256]{2,1,0:T(8,128)(2,1)S(1)} %select_bitcast_fusion.1, bf16[1,512,256]{2,1,0:T(8,128)(2,1)S(1)} %bitcast.9), kind=kLoop, calls=%fused_computation | loop fusion | flops 1179648 | bytes 2359296 | tf_op jit(solution)/shard_map/stack | solution.py:403
  (4 shorter events, 0.1 us)
Async XLA Ops:
  9.2 1.9 %collective-permute-start = (bf16[512,256]{1,0:T(8,128)(2,1)}, bf16[512,256]{1,0:T(8,128)(2,1)S(1)}, u32[]{:S(2)}, u32[]{:S(2)}) collective-permute-start(bf16[512,256]{1,0:T(8,128)(2,1)} %get-tuple-element.20), channel_id=1, source_target_pairs={{0,1},{1,0},{2,3},{3,2},{4,5},{5,4},{6,7},{7,6},{8,9},{9,8},{10,11... | collective-permute-start | bytes 786440 | tf_op jit(solution)/shard_map/ppermute | solution.py:237
  12.1 5.9 %collective-permute-start.1 = (bf16[256,256]{1,0:T(8,128)(2,1)S(1)}, bf16[256,256]{1,0:T(8,128)(2,1)S(1)}, u32[]{:S(2)}, u32[]{:S(2)}) collective-permute-start(bf16[256,256]{1,0:T(8,128)(2,1)S(1)} %add_convert_fusion), channel_id=1, source_target_pairs={{0,2},{1,5},{2,0},{3,7},{4,6},{5,1},{6,4},{7,3},{8,10},{9,13},{10,... | collective-permute-start | bytes 393224 | tf_op jit(solution)/shard_map/ppermute | solution.py:237
  18.9 4.4 %collective-permute-start.2 = (bf16[128,256]{1,0:T(8,128)(2,1)S(1)}, bf16[128,256]{1,0:T(8,128)(2,1)S(1)}, u32[]{:S(2)}, u32[]{:S(2)}) collective-permute-start(bf16[128,256]{1,0:T(8,128)(2,1)S(1)} %add_convert_fusion.1), channel_id=1, source_target_pairs={{0,4},{1,3},{2,6},{3,1},{4,0},{5,7},{6,2},{7,5},{8,12},{9,11},{10,... | collective-permute-start | bytes 196616 | tf_op jit(solution)/shard_map/ppermute | solution.py:237
  23.3 1.0 %copy-start = (f32[512,256]{1,0:T(8,128)S(1)}, f32[512,256]{1,0:T(8,128)}, u32[]{:S(2)}) copy-start(f32[512,256]{1,0:T(8,128)} %get-tuple-element.19.keep_ref) | copy-start | bytes 1572868
  24.3 0.8 copy-start.1
  25.2 0.7 copy-start.2
  25.9 0.7 copy-start.3
  43.2 16.8 %collective-permute-start.4 = (bf16[512,256]{1,0:T(8,128)(2,1)}, bf16[512,256]{1,0:T(8,128)(2,1)}, u32[]{:S(2)}, u32[]{:S(2)}) collective-permute-start(bf16[512,256]{1,0:T(8,128)(2,1)} %get-tuple-element.29), channel_id=1, source_target_pairs={{0,8},{24,16},{1,9},{25,17},{2,10},{26,18},{3,11},{27,19},{4,12},{... | collective-permute-start | bytes 786440 | tf_op jit(solution)/shard_map/ppermute | solution.py:361
  52.0 9.9 %collective-permute-start.8 = (bf16[512,256]{1,0:T(8,128)(2,1)}, bf16[512,256]{1,0:T(8,128)(2,1)}, u32[]{:S(2)}, u32[]{:S(2)}) collective-permute-start(bf16[512,256]{1,0:T(8,128)(2,1)} %get-tuple-element.34), channel_id=1, source_target_pairs={{0,8},{24,16},{1,9},{25,17},{2,10},{26,18},{3,11},{27,19},{4,12},{... | collective-permute-start | bytes 786440 | tf_op jit(solution)/shard_map/ppermute | solution.py:361
  58.6 7.8 %copy-start.4 = (f32[512,256]{1,0:T(8,128)S(1)}, f32[512,256]{1,0:T(8,128)}, u32[]{:S(2)}) copy-start(f32[512,256]{1,0:T(8,128)} %get-tuple-element.25) | copy-start | bytes 1572868
  58.6 7.8 %collective-permute-start.3 = (bf16[512,256]{1,0:T(8,128)(2,1)}, bf16[512,256]{1,0:T(8,128)(2,1)S(1)}, u32[]{:S(2)}, u32[]{:S(2)}) collective-permute-start(bf16[512,256]{1,0:T(8,128)(2,1)} %get-tuple-element.26), channel_id=1, source_target_pairs={{0,8},{24,16},{1,9},{25,17},{2,10},{26,18},{3,11},{27,19},{4,12},{... | collective-permute-start | bytes 786440 | tf_op jit(solution)/shard_map/ppermute | solution.py:361
  61.3 5.3 %collective-permute-start.5 = (bf16[512,256]{1,0:T(8,128)(2,1)S(1)}, bf16[512,256]{1,0:T(8,128)(2,1)S(1)}, u32[]{:S(2)}, u32[]{:S(2)}) collective-permute-start(bf16[512,256]{1,0:T(8,128)(2,1)S(1)} %reduce-precision_convert_fusion.4), channel_id=1, source_target_pairs={{8,16},{16,8},{9,17},{17,9},{10,18},{18,10},{11,19},{19,11},{12,20... | collective-permute-start | bytes 786440 | tf_op jit(solution)/shard_map/ppermute | solution.py:368
  63.1 5.5 %collective-permute-start.9 = (bf16[512,256]{1,0:T(8,128)(2,1)S(1)}, bf16[512,256]{1,0:T(8,128)(2,1)S(1)}, u32[]{:S(2)}, u32[]{:S(2)}) collective-permute-start(bf16[512,256]{1,0:T(8,128)(2,1)S(1)} %reduce-precision_convert_fusion.1), channel_id=1, source_target_pairs={{8,16},{16,8},{9,17},{17,9},{10,18},{18,10},{11,19},{19,11},{12,20... | collective-permute-start | bytes 786440 | tf_op jit(solution)/shard_map/ppermute | solution.py:368
  66.6 3.4 %collective-permute-start.6 = (bf16[512,256]{1,0:T(8,128)(2,1)S(1)}, bf16[512,256]{1,0:T(8,128)(2,1)S(1)}, u32[]{:S(2)}, u32[]{:S(2)}) collective-permute-start(bf16[512,256]{1,0:T(8,128)(2,1)S(1)} %reduce-precision_convert_fusion.5), channel_id=1, source_target_pairs={{8,16},{16,8},{9,17},{17,9},{10,18},{18,10},{11,19},{19,11},{12,20... | collective-permute-start | bytes 786440 | tf_op jit(solution)/shard_map/ppermute | solution.py:368
  67.3 15.0 %collective-permute-start.7 = (bf16[512,256]{1,0:T(8,128)(2,1)S(1)}, bf16[512,256]{1,0:T(8,128)(2,1)S(1)}, u32[]{:S(2)}, u32[]{:S(2)}) collective-permute-start(bf16[512,256]{1,0:T(8,128)(2,1)S(1)} %reduce-precision_convert_fusion.3), channel_id=1, source_target_pairs={{8,0},{16,24},{9,1},{17,25},{10,2},{18,26},{11,3},{19,27},{12,4},{... | collective-permute-start | bytes 786440 | tf_op jit(solution)/shard_map/ppermute | solution.py:376
  68.7 19.3 %collective-permute-start.10 = (bf16[512,256]{1,0:T(8,128)(2,1)S(1)}, bf16[512,256]{1,0:T(8,128)(2,1)S(1)}, u32[]{:S(2)}, u32[]{:S(2)}) collective-permute-start(bf16[512,256]{1,0:T(8,128)(2,1)S(1)} %reduce-precision_convert_fusion), channel_id=1, source_target_pairs={{8,0},{16,24},{9,1},{17,25},{10,2},{18,26},{11,3},{19,27},{12,4},{... | collective-permute-start | bytes 786440 | tf_op jit(solution)/shard_map/ppermute | solution.py:376
  82.4 9.1 %collective-permute-start.11 = (bf16[512,256]{1,0:T(8,128)(2,1)S(1)}, bf16[512,256]{1,0:T(8,128)(2,1)S(1)}, u32[]{:S(2)}, u32[]{:S(2)}) collective-permute-start(bf16[512,256]{1,0:T(8,128)(2,1)S(1)} %reduce-precision_convert_fusion.2), channel_id=1, source_target_pairs={{8,0},{16,24},{9,1},{17,25},{10,2},{18,26},{11,3},{19,27},{12,4},{... | collective-permute-start | bytes 786440 | tf_op jit(solution)/shard_map/ppermute | solution.py:376
